TPU v7x, 32 devices: a whole 2x2x4 slice. The times are simulated.
32 devices in a mesh: row: 4 (over x, core), col: 8 (over z, y).
Axes of the slice: x: 2, y: 2, z: 4, core: 2. Of those that a mesh axis runs over, the one named last changes fastest.
Arguments:
- inputs: bfloat16 [512, 8192], P('col', 'row'), may hold values from -6 to 6
- target: bfloat16 [512, 8192], P(None, 'row'), may hold values from -6 to 6
- gate_weight: bfloat16 [8192, 16384], P('row', 'col'), may hold values from -0.0625 to 0.0625
- up_weight: bfloat16 [8192, 16384], P('row', 'col'), may hold values from -0.0625 to 0.0625
- down_weight: bfloat16 [16384, 8192], P('col', 'row'), may hold values from -0.046875 to 0.046875
Outputs:
- output: bfloat16 [512, 8192], P('col', 'row')
- grad_inputs: bfloat16 [512, 8192], P('col', 'row')
- grad_gate_weight: bfloat16 [8192, 16384], P('row', 'col')
- grad_up_weight: bfloat16 [8192, 16384], P('row', 'col')
- grad_down_weight: bfloat16 [16384, 8192], P('col', 'row')
All inputs are finite; a program needn't handle non-finite values.
Results may differ from a plain program's by a relative error of at most 0.0065.
Values may be sent and summed in bfloat16 or wider, within the bound.
A program may use at most 128 MiB of HBM per device.

v0:
```python
import jax
import jax.numpy as jnp
from jax import lax
from jax.sharding import PartitionSpec as P


def contract_first(left, right):
    return lax.dot_general(
        left, right, (((0,), (0,)), ((), ())), preferred_element_type=jnp.float32
    )


def contract_last(left, right):
    return lax.dot_general(
        left, right, (((1,), (1,)), ((), ())), preferred_element_type=jnp.float32
    )


def gate_grads(hidden_grad, gate_act, up_act):
    sigma = jax.nn.sigmoid(gate_act)
    silu_val = gate_act * sigma
    grad_gate = (hidden_grad * up_act * sigma * (1.0 + gate_act * (1.0 - sigma))).astype(
        jnp.bfloat16
    )
    grad_up = (hidden_grad * silu_val).astype(jnp.bfloat16)
    return (grad_gate, grad_up)


def body(inputs, target, gate_weight, up_weight, down_weight):
    tokens_all = lax.all_gather(inputs, "col", axis=0, tiled=True)
    gate_part = jnp.dot(tokens_all, gate_weight, preferred_element_type=jnp.float32)
    up_part = jnp.dot(tokens_all, up_weight, preferred_element_type=jnp.float32)
    gate_own, up_own = (
        lax.psum_scatter(gate_part, "row", scatter_dimension=0, tiled=True),
        lax.psum_scatter(up_part, "row", scatter_dimension=0, tiled=True),
    )
    hidden_own = (jax.nn.silu(gate_own) * up_own).astype(jnp.bfloat16)
    hidden_all = lax.all_gather(hidden_own, "row", axis=0, tiled=True)
    result_part = jnp.dot(hidden_all, down_weight, preferred_element_type=jnp.float32)
    tok_col = inputs.shape[0]
    offset = lax.axis_index("col") * tok_col
    result_own = lax.psum_scatter(result_part, "col", scatter_dimension=0, tiled=True)
    target_own = lax.dynamic_slice_in_dim(target, offset, tok_col, 0)
    error_own = (result_own - target_own.astype(jnp.float32)).astype(jnp.bfloat16)
    output = result_own.astype(jnp.bfloat16)
    error_all = lax.all_gather(error_own, "col", axis=0, tiled=True)
    grad_down_weight = contract_first(hidden_all, error_all).astype(jnp.bfloat16)
    hidden_grad_part = contract_last(error_all, down_weight)
    hidden_grad = lax.psum_scatter(hidden_grad_part, "row", scatter_dimension=0, tiled=True)
    gate_grad_own, up_grad_own = gate_grads(hidden_grad, gate_own, up_own)
    gate_grad_all, up_grad_all = (
        lax.all_gather(gate_grad_own, "row", axis=0, tiled=True),
        lax.all_gather(up_grad_own, "row", axis=0, tiled=True),
    )
    grad_gate_weight = contract_first(tokens_all, gate_grad_all).astype(jnp.bfloat16)
    grad_up_weight = contract_first(tokens_all, up_grad_all).astype(jnp.bfloat16)
    input_grad_part = contract_last(gate_grad_all, gate_weight) + contract_last(
        up_grad_all, up_weight
    )
    grad_inputs = lax.psum_scatter(input_grad_part, "col", scatter_dimension=0, tiled=True).astype(
        jnp.bfloat16
    )
    return (output, grad_inputs, grad_gate_weight, grad_up_weight, grad_down_weight)


def solution(mesh):
    placed = (P("col", "row"), P(None, "row"), P("row", "col"), P("row", "col"), P("col", "row"))
    return jax.shard_map(
        body,
        mesh=mesh,
        in_specs=placed,
        out_specs=(
            P("col", "row"),
            P("col", "row"),
            P("row", "col"),
            P("row", "col"),
            P("col", "row"),
        ),
        check_vma=False,
    )
```

profile of v0, /device:TPU:0, one launch (start us, length us, event | category | flops | bytes accessed | tf_op | source)
XLA Modules:
  0.0 552.0 jit_solution(16577409739585436568)
XLA Ops:
  7.2 0.7 all-gather.6.cloned.1.call-update
  7.9 54.2 %all-gather.6.cloned.1.call-done = bf16[512,2048]{1,0:T(8,128)(2,1)} async-done(((bf16[64,2048]{1,0:T(8,128)(2,1)}), bf16[512,2048]{1,0:T(8,128)(2,1)}) %all-gather.6.cloned.1.call-update) | async-done | bytes 2097168 | tf_op jit(solution)/shard_map/all_gather | solution.py:30
  62.1 10.5 %fusion.2 = f32[512,2048]{1,0:T(8,128)} fusion(bf16[512,2048]{1,0:T(8,128)(2,1)} %all-gather.6.cloned.1.call-done, bf16[2048,2048]{1,0:T(8,128)(2,1)} %param.8), kind=kOutput, calls=%fused_computation.11 | convolution fusion | flops 4294967296 | bytes 14680064 | tf_op jit(solution)/shard_map/dot_general | solution.py:32
  72.7 0.0 reduce-scatter.6.cloned.1.call-start
  72.8 1.5 copy-done.2
  74.3 10.1 %fusion.1 = f32[512,2048]{1,0:T(8,128)} fusion(bf16[512,2048]{1,0:T(8,128)(2,1)S(1)} %copy-done.2, bf16[2048,2048]{1,0:T(8,128)(2,1)} %param.7), kind=kOutput, calls=%fused_computation.10 | convolution fusion | flops 4294967296 | bytes 14680064 | tf_op jit(solution)/shard_map/dot_general | solution.py:31
  84.3 0.0 all-gather.8.cloned.1.call-start
  84.4 31.5 %reduce-scatter.8.cloned.1.call-done = f32[128,2048]{1,0:T(8,128)} async-done(((f32[512,2048]{1,0:T(8,128)}), f32[128,2048]{1,0:T(8,128)}) %reduce-scatter.8.cloned.1.call-update) | async-done | bytes 1048592 | tf_op jit(solution)/shard_map/reduce_scatter | solution.py:35
  115.9 47.8 %reduce-scatter.6.cloned.1.call-done = f32[128,2048]{1,0:T(8,128)} async-done(((f32[512,2048]{1,0:T(8,128)}), f32[128,2048]{1,0:T(8,128)}) %reduce-scatter.6.cloned.1.call-update) | async-done | bytes 1048592 | tf_op jit(solution)/shard_map/reduce_scatter | solution.py:34
  163.7 2.6 multiply_convert_fusion.2
  166.4 22.7 %all-gather.8.cloned.1.call-done = bf16[512,2048]{1,0:T(8,128)(2,1)} async-done(((bf16[128,2048]{1,0:T(8,128)(2,1)}), bf16[512,2048]{1,0:T(8,128)(2,1)}) %all-gather.8.cloned.1.call-update) | async-done | bytes 2097168 | tf_op jit(solution)/shard_map/all_gather | solution.py:38
  189.1 10.5 %fusion.3 = f32[512,2048]{1,0:T(8,128)} fusion(bf16[512,2048]{1,0:T(8,128)(2,1)} %all-gather.8.cloned.1.call-done, bf16[2048,2048]{1,0:T(8,128)(2,1)} %param.9), kind=kOutput, calls=%fused_computation.12 | convolution fusion | flops 4294967296 | bytes 14680064 | tf_op jit(solution)/shard_map/dot_general | solution.py:39
  199.6 0.0 all-gather.10.cloned.1.call-start
  199.7 88.0 %reduce-scatter.10.cloned.1.call-done = f32[64,2048]{1,0:T(8,128)} async-done(((f32[512,2048]{1,0:T(8,128)}), f32[64,2048]{1,0:T(8,128)}) %reduce-scatter.10.cloned.1.call-update) | async-done | bytes 524304 | tf_op jit(solution)/shard_map/reduce_scatter | solution.py:42
  287.7 2.1 subtract_convert_fusion
  289.9 0.2 reduce-scatter.12.cloned.1.call-start
  290.1 49.5 %all-gather.10.cloned.1.call-done = bf16[512,2048]{1,0:T(8,128)(2,1)} async-done(((bf16[64,2048]{1,0:T(8,128)(2,1)}), bf16[512,2048]{1,0:T(8,128)(2,1)}) %all-gather.10.cloned.1.call-update) | async-done | bytes 2097168 | tf_op jit(solution)/shard_map/all_gather | solution.py:46
  339.6 10.6 %fusion.4 = f32[512,2048]{1,0:T(8,128)} fusion(bf16[512,2048]{1,0:T(8,128)(2,1)} %all-gather.10.cloned.1.call-done, bf16[2048,2048]{1,0:T(8,128)(2,1)} %param.9), kind=kOutput, calls=%fused_computation.13 | convolution fusion | flops 4294967296 | bytes 14680064 | tf_op jit(solution)/shard_map/dot_general | solution.py:14
  350.2 43.1 %reduce-scatter.12.cloned.1.call-done = f32[128,2048]{1,0:T(8,128)} async-done(((f32[512,2048]{1,0:T(8,128)}), f32[128,2048]{1,0:T(8,128)}) %reduce-scatter.12.cloned.1.call-update) | async-done | bytes 1048592 | tf_op jit(solution)/shard_map/reduce_scatter | solution.py:49
  393.3 2.7 multiply_convert_fusion
  396.1 0.7 all-gather.14.cloned.1.call-update
  396.9 22.0 %all-gather.12.cloned.1.call-done = bf16[512,2048]{1,0:T(8,128)(2,1)} async-done(((bf16[128,2048]{1,0:T(8,128)(2,1)}), bf16[512,2048]{1,0:T(8,128)(2,1)}) %all-gather.12.cloned.1.call-update) | async-done | bytes 2097168 | tf_op jit(solution)/shard_map/all_gather | solution.py:52
  418.8 10.6 %fusion.5 = f32[512,2048]{1,0:T(8,128)} fusion(bf16[512,2048]{1,0:T(8,128)(2,1)} %all-gather.12.cloned.1.call-done, bf16[2048,2048]{1,0:T(8,128)(2,1)} %param.7), kind=kOutput, calls=%fused_computation.14 | convolution fusion | flops 4294967296 | bytes 14680064 | tf_op jit(solution)/shard_map/dot_general | solution.py:14
  429.4 14.2 %all-gather.14.cloned.1.call-done = bf16[512,2048]{1,0:T(8,128)(2,1)} async-done(((bf16[128,2048]{1,0:T(8,128)(2,1)}), bf16[512,2048]{1,0:T(8,128)(2,1)}) %all-gather.14.cloned.1.call-update) | async-done | bytes 2097168 | tf_op jit(solution)/shard_map/all_gather | solution.py:53
  443.6 11.7 %convolution_add_fusion = f32[512,2048]{1,0:T(8,128)} fusion(f32[512,2048]{1,0:T(8,128)} %fusion.5, bf16[512,2048]{1,0:T(8,128)(2,1)} %all-gather.14.cloned.1.call-done, bf16[2048,2048]{1,0:T(8,128)(2,1)} %param.8), kind=kOutput, calls=%fused_computation.3 | convolution fusion | flops 4296015872 | bytes 18874368 | tf_op jit(solution)/shard_map/dot_general | solution.py:14
  455.3 10.3 %convolution_convert_fusion = bf16[2048,2048]{1,0:T(8,128)(2,1)} fusion(bf16[512,2048]{1,0:T(8,128)(2,1)} %all-gather.8.cloned.1.call-done, bf16[512,2048]{1,0:T(8,128)(2,1)} %all-gather.10.cloned.1.call-done), kind=kOutput, calls=%fused_computation.2 | convolution fusion | flops 4299161600 | bytes 12582912 | tf_op jit(solution)/shard_map/dot_general | solution.py:8
  465.7 6.8 %convert_bitcast_fusion.1 = bf16[2048,2048]{0,1:T(8,128)(2,1)} fusion(bf16[512,2048]{1,0:T(8,128)(2,1)S(1)} %copy-done.4, bf16[512,2048]{1,0:T(8,128)(2,1)S(1)} %copy-done.3), kind=kOutput, calls=%fused_computation.1 | convolution fusion | flops 4299161600 | bytes 12582912 | tf_op jit(solution)/shard_map/dot_general | solution.py:8
  472.5 12.3 %copy.10 = bf16[2048,2048]{1,0:T(8,128)(2,1)} copy(bf16[2048,2048]{0,1:T(8,128)(2,1)} %convert_bitcast_fusion.1) | data formatting | bytes 16777216
  484.8 8.4 %convert_bitcast_fusion = bf16[2048,2048]{0,1:T(8,128)(2,1)} fusion(bf16[512,2048]{1,0:T(8,128)(2,1)} %all-gather.14.cloned.1.call-done, bf16[512,2048]{1,0:T(8,128)(2,1)S(1)} %copy-done.3), kind=kOutput, calls=%fused_computation | convolution fusion | flops 4299161600 | bytes 12582912 | tf_op jit(solution)/shard_map/dot_general | solution.py:8
  493.2 12.3 %copy.11 = bf16[2048,2048]{1,0:T(8,128)(2,1)} copy(bf16[2048,2048]{0,1:T(8,128)(2,1)} %convert_bitcast_fusion) | data formatting | bytes 16777216
  505.5 37.9 %reduce-scatter.14.cloned.1.call-done = f32[64,2048]{1,0:T(8,128)} async-done(((f32[512,2048]{1,0:T(8,128)}), f32[64,2048]{1,0:T(8,128)}) %reduce-scatter.14.cloned.1.call-update) | async-done | bytes 524304 | tf_op jit(solution)/shard_map/reduce_scatter | solution.py:60
  543.4 1.8 convert_element_type.42
  (23 shorter events, 0.4 us)
Async XLA Ops:
  7.2 55.0 %all-gather.6.cloned.1.call-start = ((), (), s32[]{:S(2)}) async-start(), calls=%async_computation.5 | async-start | bytes 2359296 | tf_op jit(solution)/shard_map/all_gather | solution.py:30
  7.9 108.0 %reduce-scatter.8.cloned.1.call-start = ((), (), s32[]{:S(2)}) async-start(), calls=%async_computation.7 | async-start | bytes 5242880 | tf_op jit(solution)/shard_map/reduce_scatter | solution.py:35
  72.7 1.6 copy-start.2
  72.7 91.0 %reduce-scatter.6.cloned.1.call-start = ((), (), s32[]{:S(2)}) async-start(), calls=%async_computation.6 | async-start | bytes 5242880 | tf_op jit(solution)/shard_map/reduce_scatter | solution.py:34
  84.3 104.7 %all-gather.8.cloned.1.call-start = ((), (), s32[]{:S(2)}) async-start(), calls=%async_computation.8 | async-start | bytes 2621440 | tf_op jit(solution)/shard_map/all_gather | solution.py:38
  166.4 121.3 %reduce-scatter.10.cloned.1.call-start = ((), (), s32[]{:S(2)}) async-start(), calls=%async_computation.9 | async-start | bytes 4718592 | tf_op jit(solution)/shard_map/reduce_scatter | solution.py:42
  199.6 139.9 %all-gather.10.cloned.1.call-start = ((), (), s32[]{:S(2)}) async-start(), calls=%async_computation.10 | async-start | bytes 2359296 | tf_op jit(solution)/shard_map/all_gather | solution.py:46
  289.9 103.5 %reduce-scatter.12.cloned.1.call-start = ((), (), s32[]{:S(2)}) async-start(), calls=%async_computation.11 | async-start | bytes 5242880 | tf_op jit(solution)/shard_map/reduce_scatter | solution.py:49
  350.1 43.2 %copy-start = (f32[128,2048]{1,0:T(8,128)S(1)}, f32[128,2048]{1,0:T(8,128)}, u32[]{:S(2)}) copy-start(f32[128,2048]{1,0:T(8,128)} %reduce-scatter.8.cloned.1.call-done) | copy-start | bytes 3145732
  350.1 43.2 %copy-start.1 = (f32[128,2048]{1,0:T(8,128)S(1)}, f32[128,2048]{1,0:T(8,128)}, u32[]{:S(2)}) copy-start(f32[128,2048]{1,0:T(8,128)} %reduce-scatter.6.cloned.1.call-done) | copy-start | bytes 3145732
  350.2 68.7 %all-gather.12.cloned.1.call-start = ((), (), s32[]{:S(2)}) async-start(), calls=%async_computation.12 | async-start | bytes 2621440 | tf_op jit(solution)/shard_map/all_gather | solution.py:52
  396.1 47.5 %all-gather.14.cloned.1.call-start = ((), (), s32[]{:S(2)}) async-start(), calls=%async_computation.13 | async-start | bytes 2621440 | tf_op jit(solution)/shard_map/all_gather | solution.py:53
  396.8 146.5 %reduce-scatter.14.cloned.1.call-start = ((), (), s32[]{:S(2)}) async-start(), calls=%async_computation.14 | async-start | bytes 4718592 | tf_op jit(solution)/shard_map/reduce_scatter | solution.py:60
  455.3 10.4 %copy-start.3 = (bf16[512,2048]{1,0:T(8,128)(2,1)S(1)}, bf16[512,2048]{1,0:T(8,128)(2,1)}, u32[]{:S(2)}) copy-start(bf16[512,2048]{1,0:T(8,128)(2,1)} %all-gather.6.cloned.1.call-done) | copy-start | bytes 6291460
  455.3 10.4 %copy-start.4 = (bf16[512,2048]{1,0:T(8,128)(2,1)S(1)}, bf16[512,2048]{1,0:T(8,128)(2,1)}, u32[]{:S(2)}) copy-start(bf16[512,2048]{1,0:T(8,128)(2,1)} %all-gather.12.cloned.1.call-done) | copy-start | bytes 6291460
Sparse Core Ops, SparseCore 0:
  10.1 51.9 all-gather.5
  72.8 43.0 reduce-scatter.7
  119.1 44.5 reduce-scatter.5
  166.5 22.5 all-gather.7
  199.8 87.8 reduce-scatter.9
  290.5 49.0 all-gather.9
  350.3 42.9 reduce-scatter.11
  396.2 22.5 all-gather.11
  421.0 22.5 all-gather.13
  455.4 87.9 reduce-scatter.13
where the time goes:
time: 553 us; the launch traced here: 552 us
  waiting for transfers between devices  412 us (75%)
  matrix products  89.5 us (16%)
  local copies, waits for them, and re-layouts  26.1 us (5%)
  between operations  14.2 us (3%)
  other arithmetic  9.27 us (2%)
    reduce_scatter x1, waiting for transfers between devices, body(): lax.psum_scatter(result_part, 'col', scatter_dimension=0, tiled=True)  88 us
    all_gather x1, waiting for transfers between devices, body(): tokens_all = lax.all_gather(inputs, 'col', axis=0, tiled=True)  54.2 us
    all_gather x1, waiting for transfers between devices, body(): error_all = lax.all_gather(error_own, 'col', axis=0, tiled=True)  49.5 us
    reduce_scatter x1, waiting for transfers between devices, body(): lax.psum_scatter(gate_part, 'row', scatter_dimension=0, tiled=True)  47.8 us
    reduce_scatter x1, waiting for transfers between devices, body(): lax.psum_scatter(hidden_grad_part, 'row', scatter_dimension=0, tiled=True)  43.1 us
    reduce_scatter x1, waiting for transfers between devices, body(): lax.psum_scatter(input_grad_part, 'col', scatter_dimension=0, tiled=True)  37.9 us
    dot_general x3, matrix products, contract_last(): lax.dot_general(left, right, (((1,), (1,)), ((), ())), preferred_element_...  32.8 us
    reduce_scatter x1, waiting for transfers between devices, body(): lax.psum_scatter(up_part, 'row', scatter_dimension=0, tiled=True)  31.5 us
  transfers between devices with their start and end apart: 10, of which 10 were waited for; matrix products, arithmetic and copies ran while one was open for 13% of the time, Pallas kernels for 0%

commit v1 on v0

v1 whole, which is shorter than its diff:
```python
import functools

import jax
import jax.numpy as jnp
from jax import lax
from jax.experimental import pallas as pl
from jax.experimental.pallas import tpu as pltpu
from jax.sharding import PartitionSpec as P

BF = jnp.bfloat16
F32 = jnp.float32
CHUNKS = 4
LAG = 4
MESH = pl.DeviceIdType.MESH


class Group:
    def __init__(self, axis, size, other):
        self.axis = axis
        self.line_size = size // 2
        me = lax.axis_index(axis)
        self.pair = lax.rem(me, 2)
        self.line = lax.div(me, 2)
        self.other = lax.axis_index(other)

    def device(self, line, pair):
        at = line * 2 + pair
        return (at, self.other) if self.axis == "row" else (self.other, at)

    def mate(self):
        return self.device(self.line, 1 - self.pair)

    def ahead(self, d):
        return lax.rem(self.line + d, self.line_size)


class Comm:
    def __init__(self, group, send, recv, sent):
        self.g, self.send, self.recv, self.sent = group, send, recv, sent

    def start(self, k, slot, src, dst, dst_slot, device):
        copy = pltpu.make_async_remote_copy(
            src_ref=src,
            dst_ref=dst,
            send_sem=self.send.at[k, slot],
            recv_sem=self.recv.at[k, dst_slot],
            device_id=device,
            device_id_type=MESH,
        )
        copy.start()
        self.sent.append(copy)

    def arrived(self, k, slot, ref):
        pltpu.make_async_remote_copy(
            src_ref=ref,
            dst_ref=ref,
            send_sem=self.send.at[k, slot],
            recv_sem=self.recv.at[k, slot],
            device_id=self.g.mate(),
            device_id_type=MESH,
        ).wait_recv()


class Gather(Comm):
    def spread(self, buf, k, src=None):
        g = self.g
        own = buf.at[k, g.pair, g.line]
        for d in range(1, g.line_size):
            self.start(k, d - 1, own if src is None else src, own, g.line_size - 1 - d, g.device(g.ahead(d), g.pair))

    def forward(self, buf, k):
        g = self.g
        for e in range(g.line_size - 1):
            self.arrived(k, e, buf.at[k, g.pair, g.ahead(1 + e)])
        half = buf.at[k, g.pair]
        self.start(k, g.line_size - 1, half, half, g.line_size - 1, g.mate())

    def finish(self, buf, k):
        self.arrived(k, self.g.line_size - 1, buf.at[k, 1 - self.g.pair])


class Scatter(Comm):
    def exchange(self, part, from_mate, k):
        g = self.g
        self.start(k, g.line_size - 1, part.at[k, 1 - g.pair], from_mate.at[k], g.line_size - 1, g.mate())

    def pass_on(self, part, from_mate, from_line, k):
        g = self.g
        self.arrived(k, g.line_size - 1, from_mate.at[k])
        for d in range(1, g.line_size):
            to = g.ahead(d)
            mine = part.at[k, g.pair, to]
            mine[...] = (mine[...].astype(F32) + from_mate[k, to].astype(F32)).astype(BF)
            slot = g.line_size - 1 - d
            self.start(k, d - 1, mine, from_line.at[k, slot], slot, g.device(to, g.pair))

    def landed(self, from_line, k):
        for e in range(self.g.line_size - 1):
            self.arrived(k, e, from_line.at[k, e])

    def total(self, part, from_mate, from_line, k, cols=slice(None)):
        g = self.g
        acc = part[k, g.pair, g.line, :, cols].astype(F32) + from_mate[k, g.line, :, cols].astype(F32)
        for e in range(g.line_size - 1):
            acc = acc + from_line[k, e, :, cols].astype(F32)
        return acc


def flat(value):
    return value.reshape(-1, value.shape[-1])


def tile_of(size):
    return 256 if size % 256 == 0 else 128


def last_last(left, right):
    return lax.dot_general(left, right, (((1,), (1,)), ((), ())), preferred_element_type=F32)


def layer_kernel(
    rows_n, cols_n,
    x_ref, target_hbm, wg_hbm, wu_hbm, wd_hbm,
    out_ref, gx_ref, tok_hbm, hid_hbm, err_hbm, grad_hbm,
    wg, wu, wd, target, tok, hid, err, grad,
    p1, m1, l1, p2, m2, l2, p3, m3, l3, p4, m4, l4,
    row_send, row_recv, col_send, col_recv, load_sem, store_sem,
):
    hidden = wg.shape[1]
    feats = wg.shape[0]
    chunks = tok.shape[0]
    tb = tok.shape[3]
    row = Group("row", rows_n, "col")
    col = Group("col", cols_n, "row")

    loads = [
        pltpu.make_async_copy(wg_hbm, wg, load_sem.at[0]),
        pltpu.make_async_copy(wu_hbm, wu, load_sem.at[1]),
        pltpu.make_async_copy(wd_hbm, wd, load_sem.at[2]),
        pltpu.make_async_copy(
            target_hbm.at[pl.ds(pl.multiple_of(lax.axis_index("col") * tb * chunks, tb * chunks), tb * chunks)],
            target, load_sem.at[3],
        ),
    ]

    barrier = pltpu.get_barrier_semaphore()
    peers = []
    for g in (row, col):
        peers.append(g.mate())
        for d in range(1, g.line_size):
            peers.append(g.device(g.ahead(d), g.pair))
    for peer in peers:
        pl.semaphore_signal(barrier, inc=1, device_id=peer, device_id_type=MESH)
    pl.semaphore_wait(barrier, len(peers))

    sent, stores = [], []
    ag_in = Gather(col, col_send.at[0], col_recv.at[0], sent)
    rs_act = Scatter(row, row_send.at[0], row_recv.at[0], sent)
    ag_hid = Gather(row, row_send.at[1], row_recv.at[1], sent)
    rs_out = Scatter(col, col_send.at[1], col_recv.at[1], sent)
    ag_err = Gather(col, col_send.at[2], col_recv.at[2], sent)
    rs_hid = Scatter(row, row_send.at[2], row_recv.at[2], sent)
    ag_grad = Gather(row, row_send.at[3], row_recv.at[3], sent)
    rs_in = Scatter(col, col_send.at[3], col_recv.at[3], sent)

    def store(buf, out, i, k):
        copy = pltpu.make_async_copy(buf.at[k], out.at[k], store_sem.at[i, k])
        copy.start()
        stores.append(copy)

    waited = set()

    def need(i):
        if i not in waited:
            waited.add(i)
            loads[i].wait()

    def tiles(size, body):
        t = tile_of(size)

        def step(j, _):
            body(pl.ds(pl.multiple_of(j * t, t), t), j * t)
            return 0

        lax.fori_loop(0, size // t, step, 0)

    def put(part, k, cols, value):
        shape = part.shape[1:4] + (value.shape[-1],)
        part[k, :, :, :, cols] = value.astype(BF).reshape(shape)

    def token_rows(k):
        return pl.ds(k * tb, tb)

    def s_in(k):
        tok[k, col.pair, col.line] = x_ref[token_rows(k), :]
        ag_in.spread(tok, k, x_ref.at[token_rows(k)])

    def s_in_fwd(k):
        ag_in.forward(tok, k)

    def s_act(k):
        ag_in.finish(tok, k)
        need(0)
        need(1)

        def body(cols, at):
            t = cols.size
            put(p1, k, cols, jnp.dot(flat(tok[k]), wg[:, cols], preferred_element_type=F32))
            ups = pl.ds(pl.multiple_of(hidden + at, t), t)
            put(p1, k, ups, jnp.dot(flat(tok[k]), wu[:, cols], preferred_element_type=F32))

        tiles(hidden, body)
        rs_act.exchange(p1, m1, k)
        store(tok, tok_hbm, 0, k)

    def s_act_pass(k):
        rs_act.pass_on(p1, m1, l1, k)

    def s_hid(k):
        rs_act.landed(l1, k)
        gate = rs_act.total(p1, m1, l1, k, pl.ds(0, hidden))
        up = rs_act.total(p1, m1, l1, k, pl.ds(hidden, hidden))
        hid[k, row.pair, row.line] = (gate * jax.nn.sigmoid(gate) * up).astype(BF)
        ag_hid.spread(hid, k)

    def s_hid_fwd(k):
        ag_hid.forward(hid, k)

    def s_out(k):
        ag_hid.finish(hid, k)
        need(2)
        tiles(feats, lambda cols, at: put(
            p2, k, cols, jnp.dot(flat(hid[k]), wd[:, cols], preferred_element_type=F32)))
        rs_out.exchange(p2, m2, k)
        store(hid, hid_hbm, 1, k)

    def s_out_pass(k):
        rs_out.pass_on(p2, m2, l2, k)

    def s_err(k):
        rs_out.landed(l2, k)
        need(3)
        result = rs_out.total(p2, m2, l2, k)
        out_ref[token_rows(k), :] = result.astype(BF)
        err[k, col.pair, col.line] = (result - target[token_rows(k), :].astype(F32)).astype(BF)
        ag_err.spread(err, k)

    def s_err_fwd(k):
        ag_err.forward(err, k)

    def s_ghid(k):
        ag_err.finish(err, k)
        tiles(hidden, lambda cols, at: put(p3, k, cols, last_last(flat(err[k]), wd[cols, :])))
        rs_hid.exchange(p3, m3, k)
        store(err, err_hbm, 2, k)

    def s_ghid_pass(k):
        rs_hid.pass_on(p3, m3, l3, k)

    def s_grads(k):
        rs_hid.landed(l3, k)
        gate = rs_act.total(p1, m1, l1, k, pl.ds(0, hidden))
        up = rs_act.total(p1, m1, l1, k, pl.ds(hidden, hidden))
        dh = rs_hid.total(p3, m3, l3, k)
        sigma = jax.nn.sigmoid(gate)
        grad[k, row.pair, row.line, :, pl.ds(0, hidden)] = (
            dh * up * sigma * (1.0 + gate * (1.0 - sigma))).astype(BF)
        grad[k, row.pair, row.line, :, pl.ds(hidden, hidden)] = (dh * (gate * sigma)).astype(BF)
        ag_grad.spread(grad, k)

    def s_grads_fwd(k):
        ag_grad.forward(grad, k)

    def s_gin(k):
        ag_grad.finish(grad, k)
        tiles(feats, lambda cols, at: put(
            p4, k, cols,
            last_last(flat(grad[k, :, :, :, pl.ds(0, hidden)]), wg[cols, :])
            + last_last(flat(grad[k, :, :, :, pl.ds(hidden, hidden)]), wu[cols, :])))
        rs_in.exchange(p4, m4, k)
        store(grad, grad_hbm, 3, k)

    def s_gin_pass(k):
        rs_in.pass_on(p4, m4, l4, k)

    def s_gout(k):
        rs_in.landed(l4, k)
        gx_ref[token_rows(k), :] = rs_in.total(p4, m4, l4, k).astype(BF)

    stages = [
        s_in_fwd, s_act, s_act_pass, s_hid, s_hid_fwd, s_out, s_out_pass, s_err, s_err_fwd,
        s_ghid, s_ghid_pass, s_grads, s_grads_fwd, s_gin, s_gin_pass, s_gout,
    ]
    for k in range(chunks):
        s_in(k)
    for copy in loads:
        copy.start()
    order = sorted((s + LAG * k, -s, k, s) for k in range(chunks) for s in range(len(stages)))
    for _, _, k, s in order:
        stages[s](k)
    for copy in sent:
        copy.wait_send()
    for copy in stores:
        copy.wait()


def run_layer(rows_n, cols_n, inputs, target, gate_weight, up_weight, down_weight):
    own, feats = inputs.shape
    hidden = gate_weight.shape[1]
    chunks = CHUNKS
    while chunks > 1 and (own % (16 * chunks) or (own * cols_n) % (16 * chunks * rows_n)):
        chunks //= 2
    tb = own // chunks
    rb = own * cols_n // chunks // rows_n
    rl, cl = rows_n // 2, cols_n // 2

    def by_col(width):
        return (chunks, 2, cl, tb, width)

    def by_row(width):
        return (chunks, 2, rl, rb, width)

    def scatter_bufs(line, rows, width):
        return [
            pltpu.VMEM((chunks, 2, line, rows, width), BF),
            pltpu.VMEM((chunks, line, rows, width), BF),
            pltpu.VMEM((chunks, line - 1, rows, width), BF),
        ]

    anywhere = pl.BlockSpec(memory_space=pl.ANY)
    vmem = pl.BlockSpec(memory_space=pltpu.VMEM)
    kept = [by_col(feats), by_row(hidden), by_col(feats), by_row(2 * hidden)]
    return pl.pallas_call(
        functools.partial(layer_kernel, rows_n, cols_n),
        out_shape=[jax.ShapeDtypeStruct((own, feats), BF)] * 2 + [jax.ShapeDtypeStruct(s, BF) for s in kept],
        in_specs=[vmem] + [anywhere] * 4,
        out_specs=[vmem] * 2 + [anywhere] * 4,
        scratch_shapes=[
            pltpu.VMEM(gate_weight.shape, BF),
            pltpu.VMEM(up_weight.shape, BF),
            pltpu.VMEM(down_weight.shape, BF),
            pltpu.VMEM((own, feats), BF),
            *[pltpu.VMEM(s, BF) for s in kept],
            *scatter_bufs(rl, rb, 2 * hidden),
            *scatter_bufs(cl, tb, feats),
            *scatter_bufs(rl, rb, hidden),
            *scatter_bufs(cl, tb, feats),
            pltpu.SemaphoreType.DMA((4, chunks, rl)),
            pltpu.SemaphoreType.DMA((4, chunks, rl)),
            pltpu.SemaphoreType.DMA((4, chunks, cl)),
            pltpu.SemaphoreType.DMA((4, chunks, cl)),
            pltpu.SemaphoreType.DMA((4,)),
            pltpu.SemaphoreType.DMA((4, chunks)),
        ],
        compiler_params=pltpu.CompilerParams(
            collective_id=0, has_side_effects=True, vmem_limit_bytes=60 * 2**20
        ),
        cost_estimate=pl.CostEstimate(
            flops=12 * own * cols_n * feats * hidden,
            bytes_accessed=6 * feats * hidden,
            transcendentals=0,
        ),
        name="layer",
    )(inputs, target, gate_weight, up_weight, down_weight)


def outer_kernel(n, left_ref, *refs):
    turned = left_ref[...].T
    for right_ref, out_ref in zip(refs[:n], refs[n:]):
        out_ref[...] = jnp.dot(turned, right_ref[...], preferred_element_type=F32).astype(BF)


def outer_products(left, rights):
    tokens, wide = left.shape
    step = 256 if wide % 256 == 0 else 128
    width = rights[0][2]
    return pl.pallas_call(
        functools.partial(outer_kernel, len(rights)),
        grid=(wide // step,),
        out_shape=[jax.ShapeDtypeStruct((wide, width), BF)] * len(rights),
        in_specs=[pl.BlockSpec((tokens, step), lambda i: (0, i))]
        + [pl.BlockSpec((tokens, width), functools.partial(lambda at, i: (0, at), at)) for _, at, _ in rights],
        out_specs=[pl.BlockSpec((step, width), lambda i: (i, 0))] * len(rights),
        compiler_params=pltpu.CompilerParams(vmem_limit_bytes=48 * 2**20),
        name="outer",
    )(left, *[r for r, _, _ in rights])


def body(rows_n, cols_n, inputs, target, gate_weight, up_weight, down_weight):
    output, grad_inputs, tok, hid, err, grad = run_layer(
        rows_n, cols_n, inputs, target, gate_weight, up_weight, down_weight)
    tok, hid, err, grad = (flat(a) for a in (tok, hid, err, grad))
    hidden = gate_weight.shape[1]
    grad_gate_weight, grad_up_weight = outer_products(tok, [(grad, 0, hidden), (grad, 1, hidden)])
    (grad_down_weight,) = outer_products(hid, [(err, 0, err.shape[1])])
    return (output, grad_inputs, grad_gate_weight, grad_up_weight, grad_down_weight)


def solution(mesh):
    placed = (P("col", "row"), P(None, "row"), P("row", "col"), P("row", "col"), P("col", "row"))
    return jax.shard_map(
        functools.partial(body, mesh.shape["row"], mesh.shape["col"]),
        mesh=mesh,
        in_specs=placed,
        out_specs=(
            P("col", "row"),
            P("col", "row"),
            P("row", "col"),
            P("row", "col"),
            P("col", "row"),
        ),
        check_vma=False,
    )
```

time: 553 us -> 248 us (0.45)
  waiting for transfers between devices: 412 us -> 0 us
  Pallas kernels: 0 us -> 244 us
  matrix products: 89.5 us -> 0 us
  local copies, waits for them, and re-layouts: 26.1 us -> 3 us
  between operations: 14.2 us -> 0.66 us
  other arithmetic: 9.27 us -> 0 us
    reduce_scatter x5 -> x0, waiting for transfers between devices: 248 us -> none  [the longest x1 88 us: body(): lax.psum_scatter(result_part, 'col', scatter_dimension=0, tiled=True)]
    pallas_call x0 -> x3, Pallas kernels: none -> 244 us  [the longest x1 223 us: run_layer(): pl.pallas_call(functools.partial(layer_kernel, rows_n, cols_n), out_shape...]
    all_gather x5 -> x0, waiting for transfers between devices: 163 us -> none  [the longest x1 54.2 us: body(): tokens_all = lax.all_gather(inputs, 'col', axis=0, tiled=True)]
    dot_general x9 -> x0, matrix products: 89.5 us -> none  [the longest x3 32.8 us: contract_last(): lax.dot_general(left, right, (((1,), (1,)), ((), ())), preferred_element_...]
    unnamed x12, local copies, waits for them, and re-layouts: 26.1 us -> 3 us
    convert_element_type x4 -> x0, other arithmetic: 9.27 us -> none  [the longest x1 2.74 us: gate_grads(): grad_up = (hidden_grad * silu_val).astype(jnp.bfloat16)]
  transfers between devices with their start and end apart: 10 -> 0, of which waited for: 10 -> 0; matrix products, arithmetic and copies ran while one was open for 13% -> 0% of each run, Pallas kernels for 0% -> 0%
where the time goes in v1:
time: 248 us
  Pallas kernels  244 us (98%)
  local copies, waits for them, and re-layouts  3 us (1%)
    pallas_call x1, Pallas kernels, run_layer(): pl.pallas_call(functools.partial(layer_kernel, rows_n, cols_n), out_shape...  223 us
    pallas_call x2, Pallas kernels, outer_products(): pl.pallas_call(functools.partial(outer_kernel, len(rights)), grid=(wide /...  21.7 us

profile of v1, /device:TPU:0, one launch (start us, length us, event | category | flops | bytes accessed | tf_op | source)
XLA Modules:
  0.0 248.1 jit_solution(11116177337577349326)
XLA Ops:
  0.6 222.8 %layer.1 = (bf16[64,2048]{1,0:T(8,128)(2,1)}, bf16[64,2048]{1,0:T(8,128)(2,1)}, bf16[4,2,4,16,2048]{4,3,2,1,0:T(8,128)(2,1)}, bf16[4,2,2,32,2048]{4,3,2,1,0:T(8,...) custom-call(bf16[64,2048]{1,0:T(8,128)(2,1)} %x_ref.1, ...), custom_call_target="tpu_custom_call" | custom-call | flops 25769803776 | bytes 25165824 | tf_op jit(solution)/shard_map/layer/pallas_call | solution.py:333
  223.4 0.0 copy-start
  223.4 1.6 copy-done
  225.0 0.0 copy-start.1
  225.0 0.0 copy-start.2
  225.0 13.9 %outer.2 = (bf16[2048,2048]{1,0:T(8,128)(2,1)}, bf16[2048,2048]{1,0:T(8,128)(2,1)}) custom-call(bf16[512,2048]{1,0:T(8,128)(2,1)S(1)} %bitcast.4, bf16[512,4096]{1,0:T(8,128)(2,1)} %bitcast.7, bf16[512,4096]{1,0:T(8,128)(2,1)} %bitcast.8), custom_call_target="tpu_custom_call" | custom-call | tf_op jit(solution)/shard_map/outer/pallas_call | solution.py:377
  238.9 0.0 copy-start.4
  238.9 0.0 copy-start.3
  239.0 0.0 copy-done.1
  239.0 0.0 copy-done.2
  239.0 7.8 %outer.3 = bf16[2048,2048]{1,0:T(8,128)(2,1)} custom-call(bf16[512,2048]{1,0:T(8,128)(2,1)S(1)} %bitcast.5, bf16[512,2048]{1,0:T(8,128)(2,1)S(1)} %bitcast.6), custom_call_target="tpu_custom_call" | custom-call | tf_op jit(solution)/shard_map/outer/pallas_call | solution.py:377
  246.7 0.0 copy-done.4
  246.7 0.7 copy.12
  247.4 0.0 copy-done.3
  247.4 0.7 copy.13
Async XLA Ops:
  223.4 1.6 copy-start
  225.0 14.0 %copy-start.1 = (bf16[4,2,2,32,2048]{4,3,2,1,0:T(8,128)(2,1)S(1)}, bf16[4,2,2,32,2048]{4,3,2,1,0:T(8,128)(2,1)}, u32[]{:S(2)}) copy-start(bf16[4,2,2,32,2048]{4,3,2,1,0:T(8,128)(2,1)} %get-tuple-element.19) | copy-start | bytes 6291460
  225.0 14.0 %copy-start.2 = (bf16[4,2,4,16,2048]{4,3,2,1,0:T(8,128)(2,1)S(1)}, bf16[4,2,4,16,2048]{4,3,2,1,0:T(8,128)(2,1)}, u32[]{:S(2)}) copy-start(bf16[4,2,4,16,2048]{4,3,2,1,0:T(8,128)(2,1)} %get-tuple-element.20) | copy-start | bytes 6291460
  238.9 7.8 %copy-start.4 = (bf16[64,2048]{1,0:T(8,128)(2,1)S(1)}, bf16[64,2048]{1,0:T(8,128)(2,1)}, u32[]{:S(2)}) copy-start(bf16[64,2048]{1,0:T(8,128)(2,1)} %get-tuple-element.26) | copy-start | bytes 786436
  238.9 8.5 %copy-start.3 = (bf16[64,2048]{1,0:T(8,128)(2,1)S(1)}, bf16[64,2048]{1,0:T(8,128)(2,1)}, u32[]{:S(2)}) copy-start(bf16[64,2048]{1,0:T(8,128)(2,1)} %get-tuple-element.27) | copy-start | bytes 786436

commit v2 on v1

--- a/solution.py
+++ b/solution.py
@@ -10,7 +10,7 @@
 BF = jnp.bfloat16
 F32 = jnp.float32
 CHUNKS = 4
-LAG = 4
+TURNS = ("0101023102103102", "1302132023132031", "2030121031230231", "0231202313210323")
 MESH = pl.DeviceIdType.MESH
 
 
@@ -62,40 +62,53 @@
 
 
 class Gather(Comm):
+    def to_mate(self, buf, k, d, src=None):
+        g = self.g
+        block = buf.at[k, g.pair, g.ahead(d)]
+        slot = g.line_size - 1 + d
+        self.start(k, slot, block if src is None else src, block, slot, g.mate())
+
     def spread(self, buf, k, src=None):
         g = self.g
         own = buf.at[k, g.pair, g.line]
         for d in range(1, g.line_size):
             self.start(k, d - 1, own if src is None else src, own, g.line_size - 1 - d, g.device(g.ahead(d), g.pair))
+        self.to_mate(buf, k, 0, src)
 
     def forward(self, buf, k):
         g = self.g
-        for e in range(g.line_size - 1):
-            self.arrived(k, e, buf.at[k, g.pair, g.ahead(1 + e)])
-        half = buf.at[k, g.pair]
-        self.start(k, g.line_size - 1, half, half, g.line_size - 1, g.mate())
+        for d in range(1, g.line_size):
+            self.arrived(k, d - 1, buf.at[k, g.pair, g.ahead(d)])
+            self.to_mate(buf, k, d)
 
     def finish(self, buf, k):
-        self.arrived(k, self.g.line_size - 1, buf.at[k, 1 - self.g.pair])
+        g = self.g
+        for d in range(g.line_size):
+            self.arrived(k, g.line_size - 1 + d, buf.at[k, 1 - g.pair, g.ahead(d)])
 
 
 class Scatter(Comm):
     def exchange(self, part, from_mate, k):
         g = self.g
-        self.start(k, g.line_size - 1, part.at[k, 1 - g.pair], from_mate.at[k], g.line_size - 1, g.mate())
+        for d in [*range(1, g.line_size), 0]:
+            to = g.ahead(d)
+            slot = g.line_size - 1 + d
+            self.start(k, slot, part.at[k, 1 - g.pair, to], from_mate.at[k, to], slot, g.mate())
 
     def pass_on(self, part, from_mate, from_line, k):
         g = self.g
-        self.arrived(k, g.line_size - 1, from_mate.at[k])
         for d in range(1, g.line_size):
             to = g.ahead(d)
+            self.arrived(k, g.line_size - 1 + d, from_mate.at[k, to])
             mine = part.at[k, g.pair, to]
             mine[...] = (mine[...].astype(F32) + from_mate[k, to].astype(F32)).astype(BF)
             slot = g.line_size - 1 - d
             self.start(k, d - 1, mine, from_line.at[k, slot], slot, g.device(to, g.pair))
 
-    def landed(self, from_line, k):
-        for e in range(self.g.line_size - 1):
+    def landed(self, from_mate, from_line, k):
+        g = self.g
+        self.arrived(k, g.line_size - 1, from_mate.at[k, g.line])
+        for e in range(g.line_size - 1):
             self.arrived(k, e, from_line.at[k, e])
 
     def total(self, part, from_mate, from_line, k, cols=slice(None)):
@@ -108,6 +121,19 @@
 
 def flat(value):
     return value.reshape(-1, value.shape[-1])
+
+
+def turns(chunks, stages):
+    if chunks == 4 and stages == 16:
+        line = [int(c) for c in "".join(TURNS)]
+    else:
+        line = [k for _, _, k in sorted((s + k, -s, k) for k in range(chunks) for s in range(stages))]
+    done = [0] * chunks
+    order = []
+    for k in line:
+        order.append((k, done[k]))
+        done[k] += 1
+    return order
 
 
 def tile_of(size):
@@ -217,7 +243,7 @@
         rs_act.pass_on(p1, m1, l1, k)
 
     def s_hid(k):
-        rs_act.landed(l1, k)
+        rs_act.landed(m1, l1, k)
         gate = rs_act.total(p1, m1, l1, k, pl.ds(0, hidden))
         up = rs_act.total(p1, m1, l1, k, pl.ds(hidden, hidden))
         hid[k, row.pair, row.line] = (gate * jax.nn.sigmoid(gate) * up).astype(BF)
@@ -238,7 +264,7 @@
         rs_out.pass_on(p2, m2, l2, k)
 
     def s_err(k):
-        rs_out.landed(l2, k)
+        rs_out.landed(m2, l2, k)
         need(3)
         result = rs_out.total(p2, m2, l2, k)
         out_ref[token_rows(k), :] = result.astype(BF)
@@ -258,7 +284,7 @@
         rs_hid.pass_on(p3, m3, l3, k)
 
     def s_grads(k):
-        rs_hid.landed(l3, k)
+        rs_hid.landed(m3, l3, k)
         gate = rs_act.total(p1, m1, l1, k, pl.ds(0, hidden))
         up = rs_act.total(p1, m1, l1, k, pl.ds(hidden, hidden))
         dh = rs_hid.total(p3, m3, l3, k)
@@ -284,7 +310,7 @@
         rs_in.pass_on(p4, m4, l4, k)
 
     def s_gout(k):
-        rs_in.landed(l4, k)
+        rs_in.landed(m4, l4, k)
         gx_ref[token_rows(k), :] = rs_in.total(p4, m4, l4, k).astype(BF)
 
     stages = [
@@ -295,8 +321,7 @@
         s_in(k)
     for copy in loads:
         copy.start()
-    order = sorted((s + LAG * k, -s, k, s) for k in range(chunks) for s in range(len(stages)))
-    for _, _, k, s in order:
+    for k, s in turns(chunks, len(stages)):
         stages[s](k)
     for copy in sent:
         copy.wait_send()
@@ -345,10 +370,10 @@
             *scatter_bufs(cl, tb, feats),
             *scatter_bufs(rl, rb, hidden),
             *scatter_bufs(cl, tb, feats),
-            pltpu.SemaphoreType.DMA((4, chunks, rl)),
-            pltpu.SemaphoreType.DMA((4, chunks, rl)),
-            pltpu.SemaphoreType.DMA((4, chunks, cl)),
-            pltpu.SemaphoreType.DMA((4, chunks, cl)),
+            pltpu.SemaphoreType.DMA((4, chunks, 2 * rl - 1)),
+            pltpu.SemaphoreType.DMA((4, chunks, 2 * rl - 1)),
+            pltpu.SemaphoreType.DMA((4, chunks, 2 * cl - 1)),
+            pltpu.SemaphoreType.DMA((4, chunks, 2 * cl - 1)),
             pltpu.SemaphoreType.DMA((4,)),
             pltpu.SemaphoreType.DMA((4, chunks)),
         ],
@@ -372,7 +397,7 @@
 
 def outer_products(left, rights):
     tokens, wide = left.shape
-    step = 256 if wide % 256 == 0 else 128
+    step = next(t for t in (512, 256, 128) if wide % t == 0)
     width = rights[0][2]
     return pl.pallas_call(
         functools.partial(outer_kernel, len(rights)),

time: 248 us -> 188 us (0.76)
  Pallas kernels: 244 us -> 184 us
    pallas_call x1, Pallas kernels: 223 us -> 164 us  [run_layer(): pl.pallas_call(functools.partial(layer_kernel, rows_n, cols_n), out_shape...]
where the time goes in v2:
time: 188 us; the launch traced here: 187 us
  Pallas kernels  184 us (98%)
  local copies, waits for them, and re-layouts  3 us (2%)
    pallas_call x1, Pallas kernels, run_layer(): pl.pallas_call(functools.partial(layer_kernel, rows_n, cols_n), out_shape...  164 us
    pallas_call x2, Pallas kernels, outer_products(): pl.pallas_call(functools.partial(outer_kernel, len(rights)), grid=(wide /...  20.1 us

profile of v2, /device:TPU:0, one launch (start us, length us, event | category | flops | bytes accessed | tf_op | source)
XLA Modules:
  0.0 187.5 jit_solution(13163864261815137500)
XLA Ops:
  0.6 163.8 %layer.1 = (bf16[64,2048]{1,0:T(8,128)(2,1)}, bf16[64,2048]{1,0:T(8,128)(2,1)}, bf16[4,2,4,16,2048]{4,3,2,1,0:T(8,128)(2,1)}, bf16[4,2,2,32,2048]{4,3,2,1,0:T(8,...) custom-call(bf16[64,2048]{1,0:T(8,128)(2,1)} %x_ref.1, ...), custom_call_target="tpu_custom_call" | custom-call | flops 25769803776 | bytes 25165824 | tf_op jit(solution)/shard_map/layer/pallas_call | solution.py:358
  164.4 0.0 copy-start
  164.4 1.6 copy-done
  166.0 0.0 copy-start.1
  166.0 0.0 copy-start.2
  166.0 13.4 %outer.2 = (bf16[2048,2048]{1,0:T(8,128)(2,1)}, bf16[2048,2048]{1,0:T(8,128)(2,1)}) custom-call(bf16[512,2048]{1,0:T(8,128)(2,1)S(1)} %bitcast.4, bf16[512,4096]{1,0:T(8,128)(2,1)} %bitcast.7, bf16[512,4096]{1,0:T(8,128)(2,1)} %bitcast.8), custom_call_target="tpu_custom_call" | custom-call | tf_op jit(solution)/shard_map/outer/pallas_call | solution.py:402
  179.4 0.0 copy-start.4
  179.4 0.0 copy-start.3
  179.4 0.0 copy-done.1
  179.4 0.0 copy-done.2
  179.4 6.7 %outer.3 = bf16[2048,2048]{1,0:T(8,128)(2,1)} custom-call(bf16[512,2048]{1,0:T(8,128)(2,1)S(1)} %bitcast.5, bf16[512,2048]{1,0:T(8,128)(2,1)S(1)} %bitcast.6), custom_call_target="tpu_custom_call" | custom-call | tf_op jit(solution)/shard_map/outer/pallas_call | solution.py:402
  186.1 0.0 copy-done.4
  186.1 0.7 copy.12
  186.8 0.0 copy-done.3
  186.8 0.7 copy.13
Async XLA Ops:
  164.4 1.6 copy-start
  166.0 13.4 %copy-start.1 = (bf16[4,2,2,32,2048]{4,3,2,1,0:T(8,128)(2,1)S(1)}, bf16[4,2,2,32,2048]{4,3,2,1,0:T(8,128)(2,1)}, u32[]{:S(2)}) copy-start(bf16[4,2,2,32,2048]{4,3,2,1,0:T(8,128)(2,1)} %get-tuple-element.19) | copy-start | bytes 6291460
  166.0 13.4 %copy-start.2 = (bf16[4,2,4,16,2048]{4,3,2,1,0:T(8,128)(2,1)S(1)}, bf16[4,2,4,16,2048]{4,3,2,1,0:T(8,128)(2,1)}, u32[]{:S(2)}) copy-start(bf16[4,2,4,16,2048]{4,3,2,1,0:T(8,128)(2,1)} %get-tuple-element.20) | copy-start | bytes 6291460
  179.4 6.7 %copy-start.4 = (bf16[64,2048]{1,0:T(8,128)(2,1)S(1)}, bf16[64,2048]{1,0:T(8,128)(2,1)}, u32[]{:S(2)}) copy-start(bf16[64,2048]{1,0:T(8,128)(2,1)} %get-tuple-element.26) | copy-start | bytes 786436
  179.4 7.4 %copy-start.3 = (bf16[64,2048]{1,0:T(8,128)(2,1)S(1)}, bf16[64,2048]{1,0:T(8,128)(2,1)}, u32[]{:S(2)}) copy-start(bf16[64,2048]{1,0:T(8,128)(2,1)} %get-tuple-element.27) | copy-start | bytes 786436

commit v3 on v2

--- a/solution.py
+++ b/solution.py
@@ -10,7 +10,7 @@
 BF = jnp.bfloat16
 F32 = jnp.float32
 CHUNKS = 4
-TURNS = ("0101023102103102", "1302132023132031", "2030121031230231", "0231202313210323")
+TURNS = ("0102012013020130", "1213202130231302", "0130213120213023", "13120321032132")
 MESH = pl.DeviceIdType.MESH
 
 
@@ -128,6 +128,8 @@
         line = [int(c) for c in "".join(TURNS)]
     else:
         line = [k for _, _, k in sorted((s + k, -s, k) for k in range(chunks) for s in range(stages))]
+    for _ in range(line.count(chunks - 1) - (stages - 2)):
+        line.pop(len(line) - 1 - line[::-1].index(chunks - 1))
     done = [0] * chunks
     order = []
     for k in line:
@@ -137,7 +139,7 @@
 
 
 def tile_of(size):
-    return 256 if size % 256 == 0 else 128
+    return next(t for t in (512, 256, 128) if size % t == 0)
 
 
 def last_last(left, right):
@@ -147,7 +149,7 @@
 def layer_kernel(
     rows_n, cols_n,
     x_ref, target_hbm, wg_hbm, wu_hbm, wd_hbm,
-    out_ref, gx_ref, tok_hbm, hid_hbm, err_hbm, grad_hbm,
+    out_ref, gx_ref, tok_hbm, hid_hbm, err_hbm, grad_hbm, part_hbm,
     wg, wu, wd, target, tok, hid, err, grad,
     p1, m1, l1, p2, m2, l2, p3, m3, l3, p4, m4, l4,
     row_send, row_recv, col_send, col_recv, load_sem, store_sem,
@@ -303,8 +305,13 @@
             p4, k, cols,
             last_last(flat(grad[k, :, :, :, pl.ds(0, hidden)]), wg[cols, :])
             + last_last(flat(grad[k, :, :, :, pl.ds(hidden, hidden)]), wu[cols, :])))
-        rs_in.exchange(p4, m4, k)
         store(grad, grad_hbm, 3, k)
+        if k < chunks - 1:
+            rs_in.exchange(p4, m4, k)
+            return
+        copy = pltpu.make_async_copy(p4.at[k], part_hbm, load_sem.at[4])
+        copy.start()
+        stores.append(copy)
 
     def s_gin_pass(k):
         rs_in.pass_on(p4, m4, l4, k)
@@ -357,9 +364,12 @@
     kept = [by_col(feats), by_row(hidden), by_col(feats), by_row(2 * hidden)]
     return pl.pallas_call(
         functools.partial(layer_kernel, rows_n, cols_n),
-        out_shape=[jax.ShapeDtypeStruct((own, feats), BF)] * 2 + [jax.ShapeDtypeStruct(s, BF) for s in kept],
+        out_shape=[
+            jax.ShapeDtypeStruct(s, BF)
+            for s in [(own, feats), (max(own - tb, tb), feats), *kept, by_col(feats)[1:]]
+        ],
         in_specs=[vmem] + [anywhere] * 4,
-        out_specs=[vmem] * 2 + [anywhere] * 4,
+        out_specs=[vmem] * 2 + [anywhere] * 5,
         scratch_shapes=[
             pltpu.VMEM(gate_weight.shape, BF),
             pltpu.VMEM(up_weight.shape, BF),
@@ -374,7 +384,7 @@
             pltpu.SemaphoreType.DMA((4, chunks, 2 * rl - 1)),
             pltpu.SemaphoreType.DMA((4, chunks, 2 * cl - 1)),
             pltpu.SemaphoreType.DMA((4, chunks, 2 * cl - 1)),
-            pltpu.SemaphoreType.DMA((4,)),
+            pltpu.SemaphoreType.DMA((5,)),
             pltpu.SemaphoreType.DMA((4, chunks)),
         ],
         compiler_params=pltpu.CompilerParams(
@@ -389,6 +399,22 @@
     )(inputs, target, gate_weight, up_weight, down_weight)
 
 
+def finish_scatter(part, cols_n):
+    line_n = cols_n // 2
+    me = lax.axis_index("col")
+    pair, line = lax.rem(me, 2), lax.div(me, 2)
+    theirs = lax.dynamic_index_in_dim(part, 1 - pair, 0, keepdims=False)
+    mine = lax.dynamic_index_in_dim(part, pair, 0, keepdims=False).astype(F32)
+    got = lax.ppermute(theirs, "col", [(c, c + 1 - 2 * (c % 2)) for c in range(cols_n)])
+    mine = mine + got.astype(F32)
+    total = lax.dynamic_index_in_dim(mine, line, 0, keepdims=False)
+    for d in range(1, line_n):
+        block = lax.dynamic_index_in_dim(mine, lax.rem(line + d, line_n), 0, keepdims=False).astype(BF)
+        pairs = [(c, ((c // 2 + d) % line_n) * 2 + c % 2) for c in range(cols_n)]
+        total = total + lax.ppermute(block, "col", pairs).astype(F32)
+    return total.astype(BF)
+
+
 def outer_kernel(n, left_ref, *refs):
     turned = left_ref[...].T
     for right_ref, out_ref in zip(refs[:n], refs[n:]):
@@ -407,13 +433,21 @@
         + [pl.BlockSpec((tokens, width), functools.partial(lambda at, i: (0, at), at)) for _, at, _ in rights],
         out_specs=[pl.BlockSpec((step, width), lambda i: (i, 0))] * len(rights),
         compiler_params=pltpu.CompilerParams(vmem_limit_bytes=48 * 2**20),
+        cost_estimate=pl.CostEstimate(
+            flops=2 * tokens * wide * width * len(rights),
+            bytes_accessed=2 * (tokens * wide + (tokens + wide) * width * len(rights)),
+            transcendentals=0,
+        ),
         name="outer",
     )(left, *[r for r, _, _ in rights])
 
 
 def body(rows_n, cols_n, inputs, target, gate_weight, up_weight, down_weight):
-    output, grad_inputs, tok, hid, err, grad = run_layer(
+    output, first_rows, tok, hid, err, grad, part = run_layer(
         rows_n, cols_n, inputs, target, gate_weight, up_weight, down_weight)
+    last_rows = finish_scatter(part, cols_n)
+    kept_rows = inputs.shape[0] - last_rows.shape[0]
+    grad_inputs = jnp.concatenate([first_rows[:kept_rows], last_rows], axis=0)
     tok, hid, err, grad = (flat(a) for a in (tok, hid, err, grad))
     hidden = gate_weight.shape[1]
     grad_gate_weight, grad_up_weight = outer_products(tok, [(grad, 0, hidden), (grad, 1, hidden)])

time: 188 us -> 178 us (0.947)
  Pallas kernels: 184 us -> 165 us
  starting transfers between devices: 0 us -> 6.2 us
  local copies, waits for them, and re-layouts: 3 us -> 4.9 us
    pallas_call x1, Pallas kernels: 164 us -> 145 us  [run_layer(): pl.pallas_call(functools.partial(layer_kernel, rows_n, cols_n), out_shape...]
    ppermute x0 -> x4, starting transfers between devices: none -> 6.2 us  [the longest x3 6.13 us: finish_scatter(): total = total + lax.ppermute(block, 'col', pairs).astype(F32)]
    unnamed x12 -> x13, local copies, waits for them, and re-layouts: 3 us -> 3.89 us
  transfers between devices with their start and end apart: 0 -> 4, of which waited for: 0 -> 0; matrix products, arithmetic and copies ran while one was open for 0% -> 0% of each run, Pallas kernels for 0% -> 11%
where the time goes in v3:
time: 178 us; the launch traced here: 177 us
  Pallas kernels  165 us (93%)
  starting transfers between devices  6.2 us (3%)
  local copies, waits for them, and re-layouts  4.9 us (3%)
    pallas_call x1, Pallas kernels, run_layer(): pl.pallas_call(functools.partial(layer_kernel, rows_n, cols_n), out_shape...  145 us
    pallas_call x2, Pallas kernels, outer_products(): pl.pallas_call(functools.partial(outer_kernel, len(rights)), grid=(wide /...  20 us
    ppermute x3, starting transfers between devices, finish_scatter(): total = total + lax.ppermute(block, 'col', pairs).astype(F32)  6.13 us
    unnamed x13, local copies, waits for them, and re-layouts  3.89 us
  transfers between devices with their start and end apart: 4, of which 0 were waited for; matrix products, arithmetic and copies ran while one was open for 0% of the time, Pallas kernels for 11%

profile of v3, /device:TPU:0, one launch (start us, length us, event | category | flops | bytes accessed | tf_op | source)
XLA Modules:
  0.0 177.5 jit_solution(6785991314974123150)
XLA Ops:
  0.6 144.8 %layer.1 = (bf16[64,2048]{1,0:T(8,128)(2,1)}, bf16[48,2048]{1,0:T(8,128)(2,1)}, bf16[4,2,4,16,2048]{4,3,2,1,0:T(8,128)(2,1)}, bf16[4,2,2,32,2048]{4,3,2,1,0:T(8,...) custom-call(bf16[64,2048]{1,0:T(8,128)(2,1)} %x_ref.1, ...), custom_call_target="tpu_custom_call" | custom-call | flops 25769803776 | bytes 25165824 | tf_op jit(solution)/shard_map/layer/pallas_call | solution.py:365
  145.5 1.0 dynamic-slice_bitcast_fusion
  146.4 0.1 collective-permute-start
  146.5 0.0 copy-start.2
  146.5 1.6 copy-done.2
  148.1 0.0 copy-start.3
  148.1 0.0 copy-start
  148.1 13.4 %outer.2 = (bf16[2048,2048]{1,0:T(8,128)(2,1)}, bf16[2048,2048]{1,0:T(8,128)(2,1)}) custom-call(bf16[512,2048]{1,0:T(8,128)(2,1)S(1)} %bitcast.25, bf16[512,4096]{1,0:T(8,128)(2,1)} %bitcast.26, bf16[512,4096]{1,0:T(8,128)(2,1)} %bitcast.27), custom_call_target="tpu_custom_call" | custom-call | flops 8589934592 | bytes 23068672 | tf_op jit(solution)/shard_map/outer/pallas_call | solution.py:428
  161.5 0.0 collective-permute-done
  161.5 0.0 copy-done.3
  161.5 0.1 convert_add_fusion
  161.6 0.0 copy-start.5
  161.6 5.5 %collective-permute-start.3 = (bf16[16,2048]{1,0:T(8,128)(2,1)S(1)}, bf16[16,2048]{1,0:T(8,128)(2,1)S(1)}, u32[]{:S(2)}, u32[]{:S(2)}) collective-permute-start(bf16[16,2048]{1,0:T(8,128)(2,1)S(1)} %get-tuple-element.24), channel_id=1, source_target_pairs={{0,6},{1,7},{2,0},{3,1},{4,2},{5,3},{6,4},{7,5},{8,14},{9,15},{10,... | collective-permute-start | bytes 196616 | tf_op jit(solution)/shard_map/ppermute | solution.py:414
  167.1 0.0 collective-permute-start.2
  167.1 0.6 collective-permute-start.1
  167.7 0.0 copy-done
  167.7 0.0 copy-start.1
  167.7 1.6 copy-done.1
  169.3 0.0 copy-start.4
  169.3 6.7 %outer.3 = bf16[2048,2048]{1,0:T(8,128)(2,1)} custom-call(bf16[512,2048]{1,0:T(8,128)(2,1)S(1)} %bitcast.23, bf16[512,2048]{1,0:T(8,128)(2,1)S(1)} %bitcast.24), custom_call_target="tpu_custom_call" | custom-call | flops 4294967296 | bytes 12582912 | tf_op jit(solution)/shard_map/outer/pallas_call | solution.py:428
  176.0 0.0 collective-permute-done.3
  176.0 0.0 collective-permute-done.2
  176.0 0.0 collective-permute-done.1
  176.0 0.0 copy-done.5
  176.1 0.7 pad_maximum_fusion
  176.8 0.0 copy-done.4
  176.8 0.7 copy.11
  (2 shorter events, 0.1 us)
Async XLA Ops:
  146.4 15.0 %collective-permute-start = (bf16[4,16,2048]{2,1,0:T(8,128)(2,1)S(1)}, bf16[4,16,2048]{2,1,0:T(8,128)(2,1)S(1)}, u32[]{:S(2)}, u32[]{:S(2)}) collective-permute-start(bf16[4,16,2048]{2,1,0:T(8,128)(2,1)S(1)} %dynamic-slice_bitcast_fusion), channel_id=1, source_target_pairs={{0,1},{1,0},{2,3},{3,2},{4,5},{5,4},{6,7},{7,6},{8,9},{9,8},{10,11... | collective-permute-start | bytes 786440 | tf_op jit(solution)/shard_map/ppermute | solution.py:408
  146.5 1.6 copy-start.2
  148.1 13.4 %copy-start.3 = (bf16[2,4,16,2048]{3,2,1,0:T(8,128)(2,1)S(1)}, bf16[2,4,16,2048]{3,2,1,0:T(8,128)(2,1)}, u32[]{:S(2)}) copy-start(bf16[2,4,16,2048]{3,2,1,0:T(8,128)(2,1)} %get-tuple-element.16) | copy-start | bytes 1572868
  148.1 19.6 %copy-start = (bf16[4,2,2,32,2048]{4,3,2,1,0:T(8,128)(2,1)S(1)}, bf16[4,2,2,32,2048]{4,3,2,1,0:T(8,128)(2,1)}, u32[]{:S(2)}) copy-start(bf16[4,2,2,32,2048]{4,3,2,1,0:T(8,128)(2,1)} %get-tuple-element.21) | copy-start | bytes 6291460
  161.6 14.5 %copy-start.5 = (bf16[48,2048]{1,0:T(8,128)(2,1)S(1)}, bf16[48,2048]{1,0:T(8,128)(2,1)}, u32[]{:S(2)}) copy-start(bf16[48,2048]{1,0:T(8,128)(2,1)} %get-tuple-element.15) | copy-start | bytes 589828
  161.6 14.4 %collective-permute-start.3 = (bf16[16,2048]{1,0:T(8,128)(2,1)S(1)}, bf16[16,2048]{1,0:T(8,128)(2,1)S(1)}, u32[]{:S(2)}, u32[]{:S(2)}) collective-permute-start(bf16[16,2048]{1,0:T(8,128)(2,1)S(1)} %get-tuple-element.24), channel_id=1, source_target_pairs={{0,6},{1,7},{2,0},{3,1},{4,2},{5,3},{6,4},{7,5},{8,14},{9,15},{10,... | collective-permute-start | bytes 196616 | tf_op jit(solution)/shard_map/ppermute | solution.py:414
  167.1 8.9 %collective-permute-start.2 = (bf16[16,2048]{1,0:T(8,128)(2,1)S(1)}, bf16[16,2048]{1,0:T(8,128)(2,1)S(1)}, u32[]{:S(2)}, u32[]{:S(2)}) collective-permute-start(bf16[16,2048]{1,0:T(8,128)(2,1)S(1)} %get-tuple-element.25), channel_id=1, source_target_pairs={{0,4},{1,5},{2,6},{3,7},{4,0},{5,1},{6,2},{7,3},{8,12},{9,13},{10,... | collective-permute-start | bytes 196616 | tf_op jit(solution)/shard_map/ppermute | solution.py:414
  167.1 8.9 %collective-permute-start.1 = (bf16[16,2048]{1,0:T(8,128)(2,1)S(1)}, bf16[16,2048]{1,0:T(8,128)(2,1)S(1)}, u32[]{:S(2)}, u32[]{:S(2)}) collective-permute-start(bf16[16,2048]{1,0:T(8,128)(2,1)S(1)} %get-tuple-element.23), channel_id=1, source_target_pairs={{0,2},{1,3},{2,4},{3,5},{4,6},{5,7},{6,0},{7,1},{8,10},{9,11},{10,... | collective-permute-start | bytes 196616 | tf_op jit(solution)/shard_map/ppermute | solution.py:414
  167.7 1.6 copy-start.1
  169.3 7.5 %copy-start.4 = (bf16[64,2048]{1,0:T(8,128)(2,1)S(1)}, bf16[64,2048]{1,0:T(8,128)(2,1)}, u32[]{:S(2)}) copy-start(bf16[64,2048]{1,0:T(8,128)(2,1)} %get-tuple-element.31) | copy-start | bytes 786436

commit v4 on v3

--- a/solution.py
+++ b/solution.py
@@ -400,18 +400,15 @@
 
 
 def finish_scatter(part, cols_n):
-    line_n = cols_n // 2
     me = lax.axis_index("col")
-    pair, line = lax.rem(me, 2), lax.div(me, 2)
-    theirs = lax.dynamic_index_in_dim(part, 1 - pair, 0, keepdims=False)
-    mine = lax.dynamic_index_in_dim(part, pair, 0, keepdims=False).astype(F32)
-    got = lax.ppermute(theirs, "col", [(c, c + 1 - 2 * (c % 2)) for c in range(cols_n)])
-    mine = mine + got.astype(F32)
-    total = lax.dynamic_index_in_dim(mine, line, 0, keepdims=False)
-    for d in range(1, line_n):
-        block = lax.dynamic_index_in_dim(mine, lax.rem(line + d, line_n), 0, keepdims=False).astype(BF)
-        pairs = [(c, ((c // 2 + d) % line_n) * 2 + c % 2) for c in range(cols_n)]
-        total = total + lax.ppermute(block, "col", pairs).astype(F32)
+
+    def block(c):
+        return part[lax.rem(c, 2), lax.div(c, 2)]
+
+    total = block(me).astype(F32)
+    for d in range(1, cols_n):
+        pairs = [(c, (c + d) % cols_n) for c in range(cols_n)]
+        total = total + lax.ppermute(block(lax.rem(me + d, cols_n)), "col", pairs).astype(F32)
     return total.astype(BF)
 
 
@@ -432,7 +429,7 @@
         in_specs=[pl.BlockSpec((tokens, step), lambda i: (0, i))]
         + [pl.BlockSpec((tokens, width), functools.partial(lambda at, i: (0, at), at)) for _, at, _ in rights],
         out_specs=[pl.BlockSpec((step, width), lambda i: (i, 0))] * len(rights),
-        compiler_params=pltpu.CompilerParams(vmem_limit_bytes=48 * 2**20),
+        compiler_params=pltpu.CompilerParams(vmem_limit_bytes=60 * 2**20),
         cost_estimate=pl.CostEstimate(
             flops=2 * tokens * wide * width * len(rights),
             bytes_accessed=2 * (tokens * wide + (tokens + wide) * width * len(rights)),

time: 178 us -> 183 us (1.028)
  starting transfers between devices: 6.2 us -> 11.3 us
  local copies, waits for them, and re-layouts: 4.9 us -> 1.8 us
  Pallas kernels: 165 us -> 167 us
    ppermute x4 -> x7, starting transfers between devices: 6.2 us -> 11.3 us  [finish_scatter(): lax.ppermute(block(lax.rem(me + d, cols_n)), 'col', pairs).astype(F32)]
    unnamed x13 -> x5, local copies, waits for them, and re-layouts: 3.89 us -> 0.71 us
  transfers between devices with their start and end apart: 4 -> 7, of which waited for: 0 -> 0; matrix products, arithmetic and copies ran while one was open for 0% -> 0% of each run, Pallas kernels for 11% -> 12%
where the time goes in v4:
time: 183 us; the launch traced here: 182 us
  Pallas kernels  167 us (91%)
  starting transfers between devices  11.3 us (6%)
    pallas_call x1, Pallas kernels, run_layer(): pl.pallas_call(functools.partial(layer_kernel, rows_n, cols_n), out_shape...  145 us
    pallas_call x2, Pallas kernels, outer_products(): pl.pallas_call(functools.partial(outer_kernel, len(rights)), grid=(wide /...  21.8 us
    ppermute x7, starting transfers between devices, finish_scatter(): lax.ppermute(block(lax.rem(me + d, cols_n)), 'col', pairs).astype(F32)  11.3 us
  transfers between devices with their start and end apart: 7, of which 0 were waited for; matrix products, arithmetic and copies ran while one was open for 0% of the time, Pallas kernels for 12%

profile of v4, /device:TPU:0, one launch (start us, length us, event | category | flops | bytes accessed | tf_op | source)
XLA Modules:
  0.0 182.2 jit_solution(13485937454039011084)
XLA Ops:
  0.8 144.8 %layer.1 = (bf16[64,2048]{1,0:T(8,128)(2,1)}, bf16[48,2048]{1,0:T(8,128)(2,1)}, bf16[4,2,4,16,2048]{4,3,2,1,0:T(8,128)(2,1)}, bf16[4,2,2,32,2048]{4,3,2,1,0:T(8,...) custom-call(bf16[64,2048]{1,0:T(8,128)(2,1)} %x_ref.1, ...), custom_call_target="tpu_custom_call" | custom-call | flops 25769803776 | bytes 25165824 | tf_op jit(solution)/shard_map/layer/pallas_call | solution.py:365
  145.6 1.1 dynamic-slice_bitcast_fusion.6
  146.7 4.9 %collective-permute-start.6 = (bf16[16,2048]{1,0:T(8,128)(2,1)S(1)}, bf16[16,2048]{1,0:T(8,128)(2,1)S(1)}, u32[]{:S(2)}, u32[]{:S(2)}) collective-permute-start(bf16[16,2048]{1,0:T(8,128)(2,1)S(1)} %get-tuple-element.24), channel_id=1, source_target_pairs={{0,7},{1,0},{2,1},{3,2},{4,3},{5,4},{6,5},{7,6},{8,15},{9,8},{10,9... | collective-permute-start | bytes 196616 | tf_op jit(solution)/shard_map/ppermute | solution.py:411
  151.6 0.0 collective-permute-start.5
  151.6 1.8 collective-permute-start.4
  153.4 2.1 %collective-permute-start.3 = (bf16[16,2048]{1,0:T(8,128)(2,1)S(1)}, bf16[16,2048]{1,0:T(8,128)(2,1)S(1)}, u32[]{:S(2)}, u32[]{:S(2)}) collective-permute-start(bf16[16,2048]{1,0:T(8,128)(2,1)S(1)} %get-tuple-element.27), channel_id=1, source_target_pairs={{0,4},{1,5},{2,6},{3,7},{4,0},{5,1},{6,2},{7,3},{8,12},{9,13},{10,... | collective-permute-start | bytes 196616 | tf_op jit(solution)/shard_map/ppermute | solution.py:411
  155.5 0.0 collective-permute-start.2
  155.5 13.3 %outer.2 = (bf16[2048,2048]{1,0:T(8,128)(2,1)}, bf16[2048,2048]{1,0:T(8,128)(2,1)}) custom-call(bf16[512,2048]{1,0:T(8,128)(2,1)} %bitcast.25, bf16[512,4096]{1,0:T(8,128)(2,1)} %bitcast.21, bf16[512,4096]{1,0:T(8,128)(2,1)} %bitcast.22), custom_call_target="tpu_custom_call" | custom-call | flops 8589934592 | bytes 23068672 | tf_op jit(solution)/shard_map/outer/pallas_call | solution.py:425
  168.8 0.0 copy-start.1
  168.8 0.0 collective-permute-done.6
  168.8 2.1 %collective-permute-start.1 = (bf16[16,2048]{1,0:T(8,128)(2,1)S(1)}, bf16[16,2048]{1,0:T(8,128)(2,1)S(1)}, u32[]{:S(2)}, u32[]{:S(2)}) collective-permute-start(bf16[16,2048]{1,0:T(8,128)(2,1)S(1)} %get-tuple-element.29), channel_id=1, source_target_pairs={{0,2},{1,3},{2,4},{3,5},{4,6},{5,7},{6,0},{7,1},{8,10},{9,11},{10,... | collective-permute-start | bytes 196616 | tf_op jit(solution)/shard_map/ppermute | solution.py:411
  170.9 0.0 collective-permute-done.5
  170.9 0.5 collective-permute-start
  171.3 0.0 copy-start
  171.3 8.5 %outer.3 = bf16[2048,2048]{1,0:T(8,128)(2,1)} custom-call(bf16[512,2048]{1,0:T(8,128)(2,1)} %bitcast.23, bf16[512,2048]{1,0:T(8,128)(2,1)} %bitcast.24), custom_call_target="tpu_custom_call" | custom-call | flops 4294967296 | bytes 12582912 | tf_op jit(solution)/shard_map/outer/pallas_call | solution.py:425
  179.8 0.0 collective-permute-done.4
  179.8 0.0 collective-permute-done.3
  179.8 0.0 collective-permute-done.2
  179.8 0.0 collective-permute-done.1
  179.8 0.0 collective-permute-done
  179.9 0.9 fusion.6
  180.8 0.0 copy-done.1
  180.8 0.7 pad_maximum_fusion
  181.5 0.0 copy-done
  181.5 0.7 copy.11
Async XLA Ops:
  146.7 22.1 %collective-permute-start.6 = (bf16[16,2048]{1,0:T(8,128)(2,1)S(1)}, bf16[16,2048]{1,0:T(8,128)(2,1)S(1)}, u32[]{:S(2)}, u32[]{:S(2)}) collective-permute-start(bf16[16,2048]{1,0:T(8,128)(2,1)S(1)} %get-tuple-element.24), channel_id=1, source_target_pairs={{0,7},{1,0},{2,1},{3,2},{4,3},{5,4},{6,5},{7,6},{8,15},{9,8},{10,9... | collective-permute-start | bytes 196616 | tf_op jit(solution)/shard_map/ppermute | solution.py:411
  151.6 19.3 %collective-permute-start.5 = (bf16[16,2048]{1,0:T(8,128)(2,1)S(1)}, bf16[16,2048]{1,0:T(8,128)(2,1)S(1)}, u32[]{:S(2)}, u32[]{:S(2)}) collective-permute-start(bf16[16,2048]{1,0:T(8,128)(2,1)S(1)} %get-tuple-element.25), channel_id=1, source_target_pairs={{0,6},{1,7},{2,0},{3,1},{4,2},{5,3},{6,4},{7,5},{8,14},{9,15},{10,... | collective-permute-start | bytes 196616 | tf_op jit(solution)/shard_map/ppermute | solution.py:411
  151.6 28.2 %collective-permute-start.4 = (bf16[16,2048]{1,0:T(8,128)(2,1)S(1)}, bf16[16,2048]{1,0:T(8,128)(2,1)S(1)}, u32[]{:S(2)}, u32[]{:S(2)}) collective-permute-start(bf16[16,2048]{1,0:T(8,128)(2,1)S(1)} %get-tuple-element.26), channel_id=1, source_target_pairs={{0,5},{1,6},{2,7},{3,0},{4,1},{5,2},{6,3},{7,4},{8,13},{9,14},{10,... | collective-permute-start | bytes 196616 | tf_op jit(solution)/shard_map/ppermute | solution.py:411
  153.4 26.4 %collective-permute-start.3 = (bf16[16,2048]{1,0:T(8,128)(2,1)S(1)}, bf16[16,2048]{1,0:T(8,128)(2,1)S(1)}, u32[]{:S(2)}, u32[]{:S(2)}) collective-permute-start(bf16[16,2048]{1,0:T(8,128)(2,1)S(1)} %get-tuple-element.27), channel_id=1, source_target_pairs={{0,4},{1,5},{2,6},{3,7},{4,0},{5,1},{6,2},{7,3},{8,12},{9,13},{10,... | collective-permute-start | bytes 196616 | tf_op jit(solution)/shard_map/ppermute | solution.py:411
  155.5 24.4 %collective-permute-start.2 = (bf16[16,2048]{1,0:T(8,128)(2,1)S(1)}, bf16[16,2048]{1,0:T(8,128)(2,1)S(1)}, u32[]{:S(2)}, u32[]{:S(2)}) collective-permute-start(bf16[16,2048]{1,0:T(8,128)(2,1)S(1)} %get-tuple-element.28), channel_id=1, source_target_pairs={{0,3},{1,4},{2,5},{3,6},{4,7},{5,0},{6,1},{7,2},{8,11},{9,12},{10,... | collective-permute-start | bytes 196616 | tf_op jit(solution)/shard_map/ppermute | solution.py:411
  168.8 12.0 %copy-start.1 = (bf16[48,2048]{1,0:T(8,128)(2,1)S(1)}, bf16[48,2048]{1,0:T(8,128)(2,1)}, u32[]{:S(2)}) copy-start(bf16[48,2048]{1,0:T(8,128)(2,1)} %get-tuple-element.15) | copy-start | bytes 589828
  168.8 11.1 %collective-permute-start.1 = (bf16[16,2048]{1,0:T(8,128)(2,1)S(1)}, bf16[16,2048]{1,0:T(8,128)(2,1)S(1)}, u32[]{:S(2)}, u32[]{:S(2)}) collective-permute-start(bf16[16,2048]{1,0:T(8,128)(2,1)S(1)} %get-tuple-element.29), channel_id=1, source_target_pairs={{0,2},{1,3},{2,4},{3,5},{4,6},{5,7},{6,0},{7,1},{8,10},{9,11},{10,... | collective-permute-start | bytes 196616 | tf_op jit(solution)/shard_map/ppermute | solution.py:411
  170.9 9.0 %collective-permute-start = (bf16[16,2048]{1,0:T(8,128)(2,1)S(1)}, bf16[16,2048]{1,0:T(8,128)(2,1)S(1)}, u32[]{:S(2)}, u32[]{:S(2)}) collective-permute-start(bf16[16,2048]{1,0:T(8,128)(2,1)S(1)} %get-tuple-element.23), channel_id=1, source_target_pairs={{0,1},{1,2},{2,3},{3,4},{4,5},{5,6},{6,7},{7,0},{8,9},{9,10},{10,1... | collective-permute-start | bytes 196616 | tf_op jit(solution)/shard_map/ppermute | solution.py:411
  171.3 10.2 %copy-start = (bf16[64,2048]{1,0:T(8,128)(2,1)S(1)}, bf16[64,2048]{1,0:T(8,128)(2,1)}, u32[]{:S(2)}) copy-start(bf16[64,2048]{1,0:T(8,128)(2,1)} %get-tuple-element.35) | copy-start | bytes 786436
